TPU v7x, 256 devices: a whole 4x4x8 slice. The times are simulated.
256 devices in a mesh: slot: 16 (over z, core), param: 16 (over x, y).
Axes of the slice: x: 4, y: 4, z: 8, core: 2. Of those that a mesh axis runs over, the one named last changes fastest.
Arguments:
- step_hist: float32 [16, 2097152], P('slot', 'param'), may hold values from -22 to 22
- diff_hist: float32 [16, 2097152], P('slot', 'param'), may hold values from -61 to 61
- gradient: float32 [2097152], P('param'), may hold values from -11 to 11
Outputs:
- direction: float32 [2097152], P('param')
- gram_matrix: float32 [33, 33], replicated
All inputs are finite; a program needn't handle non-finite values.
Results may differ from a plain program's by a relative error of at most 0.0003.
Values may be sent and summed in bfloat16 or wider, within the bound.
A program may use at most 320 MiB of HBM per device.

v0:
```python
import jax
import jax.numpy as jnp
from jax import lax
from jax.sharding import PartitionSpec as P

HIST = 16


def coefficients(gram_matrix):
    history = (gram_matrix.shape[0] - 1) // 2
    coeffs = jnp.zeros((2 * history + 1,), jnp.float32).at[2 * history].set(-1.0)
    alphas = [None] * history
    inverses = [None] * history
    for position in reversed(range(history)):
        inverse = 1.0 / gram_matrix[position, history + position]
        alpha_term = inverse * jnp.sum(coeffs * gram_matrix[:, position])
        coeffs = coeffs.at[history + position].add(-alpha_term)
        alphas[position] = alpha_term
        inverses[position] = inverse
    coeffs = coeffs * (
        gram_matrix[history - 1, 2 * history - 1] / gram_matrix[2 * history - 1, 2 * history - 1]
    )
    for position in range(history):
        beta_term = inverses[position] * jnp.sum(coeffs * gram_matrix[history + position, :])
        coeffs = coeffs.at[position].add(alphas[position] - beta_term)
    return coeffs


def pair_block(left, right):
    return jnp.einsum("akp,bjp->akbj", left, right, preferred_element_type=jnp.float32)


def assemble(blocks, own_slabs, grad_low, my_slot, my_start, history):
    grad_terms = jnp.einsum("akp,p->ak", own_slabs, grad_low, preferred_element_type=jnp.float32)
    grad_column = jnp.zeros((2, history), jnp.float32)
    grad_column = lax.dynamic_update_slice(grad_column, grad_terms, (jnp.int32(0), my_start))
    grad_column = grad_column.reshape(2 * history)
    grad_norm = jnp.dot(grad_low, grad_low, preferred_element_type=jnp.float32)
    grad_norm = jnp.where(my_slot == 0, grad_norm, 0.0)
    matrix = jnp.zeros((2 * history + 1, 2 * history + 1), jnp.float32)
    matrix = matrix.at[: 2 * history, : 2 * history].set(blocks.reshape(2 * history, 2 * history))
    matrix = matrix.at[: 2 * history, 2 * history].set(grad_column)
    matrix = matrix.at[2 * history, : 2 * history].set(grad_column)
    matrix = matrix.at[2 * history, 2 * history].set(grad_norm)
    return matrix


def shards(step_hist, diff_hist, gradient):
    local_count = step_hist.shape[0]
    history = HIST
    my_slot = lax.axis_index("slot")
    my_start = my_slot * local_count
    own_slabs = jnp.stack([step_hist, diff_hist]).astype(jnp.bfloat16)
    grad_low = gradient.astype(jnp.bfloat16)
    blocks = jnp.zeros((2, history, 2, history), jnp.float32)
    block = pair_block(own_slabs, lax.all_gather(own_slabs, "slot", axis=1, tiled=True))
    where = (jnp.int32(0), my_start, jnp.int32(0), jnp.int32(0))
    blocks = lax.dynamic_update_slice(blocks, block, where)
    matrix = assemble(blocks, own_slabs, grad_low, my_slot, my_start, history)
    total_params = gradient.shape[0] * lax.axis_size("param")
    matrix = matrix * (1.0 / total_params)
    gram_matrix = lax.psum(matrix, ("slot", "param"))
    coeffs = coefficients(gram_matrix)
    step_coeffs = lax.dynamic_slice_in_dim(coeffs, my_start, local_count)
    diff_coeffs = lax.dynamic_slice_in_dim(coeffs, history + my_start, local_count)
    partial_sum = jnp.dot(
        step_coeffs, step_hist, precision=lax.Precision.HIGHEST, preferred_element_type=jnp.float32
    )
    partial_sum = partial_sum + jnp.dot(
        diff_coeffs, diff_hist, precision=lax.Precision.HIGHEST, preferred_element_type=jnp.float32
    )
    summed = lax.psum(partial_sum, "slot")
    direction = summed + coeffs[2 * history] * gradient
    return (direction, gram_matrix)


def solution(mesh):
    in_specs = (P("slot", "param"), P("slot", "param"), P("param"))
    out_specs = (P("param"), P())
    return jax.shard_map(shards, mesh=mesh, in_specs=in_specs, out_specs=out_specs, check_vma=False)
```

profile of v0, /device:TPU:1, one launch (start us, length us, event | category | flops | bytes accessed | tf_op | source)
XLA Modules:
  0.0 354.4 jit_solution(518706204599392422)
XLA Ops:
  7.2 2.3 fusion.38
  9.5 2.0 pad_maximum_fusion.1
  11.6 1.8 fusion.5
  13.7 2.2 convolution_bitcast_fusion
  17.4 0.6 and_reduce_fusion
  18.1 53.7 %all-gather.2.cloned.1.call-done = bf16[2,16,131072]{2,0,1:T(2,128)(2,1)} async-done(((bf16[2,1,131072]{2,0,1:T(2,128)(2,1)}), bf16[2,16,131072]{2,0,1:T(2,128)(2,1)}) %all-gather.2.cloned.1.call-update) | async-done | bytes 8388624 | tf_op jit(solution)/shard_map/all_gather | solution.py:56
  71.8 12.2 %fusion.2 = f32[2,1,2,16]{3,0,2,1:T(2,128)S(1)} fusion(bf16[2,16,131072]{2,0,1:T(2,128)(2,1)} %all-gather.2.cloned.1.call-done, bf16[1,131072]{1,0:T(2,128)(2,1)S(1)} %get-tuple-element.499, bf16[1,131072]{1,0:T(2,128)(2,1)S(1)} %get-tuple-element.472), kind=kOutput, calls=%fused_computation.2 | convolution fusion | flops 17825792 | bytes 8913152 | tf_op jit(solution)/shard_map/akp,bjp->akbj/dot_general | solution.py:30
  84.1 2.4 dynamic_update_slice.6
  86.6 1.9 broadcast_select_fusion
  88.5 1.4 scatter.15
  90.6 76.7 %psum.14 = f32[33,33]{0,1:T(8,128)S(1)} all-reduce(f32[33,33]{0,1:T(8,128)S(1)} %broadcast_multiply_fusion), channel_id=1, replica_groups=mesh['slot'=16,'param'=16] {'slot','param'}, use_global_device_ids=true, to_apply=%region_1.2 | all-reduce | flops 1089 | bytes 8712 | tf_op jit(solution)/shard_map/psum | solution.py:62
  167.3 0.7 fusion.40
  170.7 0.7 fusion.37
  172.1 1.3 fusion.36
  174.8 1.3 fusion.34
  177.6 1.3 fusion.32
  180.3 1.3 fusion.30
  183.0 1.3 fusion.28
  185.8 1.3 fusion.26
  188.6 1.3 fusion.24
  191.4 1.4 fusion.22
  194.1 1.4 fusion.20
  196.9 1.4 fusion.18
  199.7 1.4 fusion.16
  202.6 1.4 fusion.14
  205.4 1.4 fusion.12
  208.2 1.4 fusion.10
  211.0 1.3 fusion.8
  213.8 0.6 multiply_reduce_fusion.15
  215.0 0.6 multiply_reduce_fusion.14
  216.4 0.6 multiply_reduce_fusion.13
  217.8 0.6 multiply_reduce_fusion.12
  219.3 0.6 multiply_reduce_fusion.11
  220.7 0.6 multiply_reduce_fusion.10
  222.1 0.6 multiply_reduce_fusion.9
  223.5 0.6 multiply_reduce_fusion.8
  224.9 0.6 multiply_reduce_fusion.7
  226.3 0.6 multiply_reduce_fusion.6
  227.7 0.6 multiply_reduce_fusion.5
  229.1 0.6 multiply_reduce_fusion.4
  230.5 0.6 multiply_reduce_fusion.3
  233.4 0.6 multiply_reduce_fusion.1
  234.8 0.6 multiply_reduce_fusion
  236.2 0.7 fusion.41
  236.9 2.7 multiply_add_fusion.1
  239.6 1.4 copy.20
  241.0 104.0 %all-reduce.3.cloned.1.call-done = f32[131072]{0:T(1024)} async-done(((f32[131072]{0:T(1024)}), f32[131072]{0:T(1024)}) %all-reduce.3.cloned.1.call-update) | async-done | bytes 524304 | tf_op jit(solution)/shard_map/psum | solution.py:72
  345.0 2.5 multiply_add_fusion
  (66 shorter events, 7.8 us)
Async XLA Ops:
  7.2 10.3 %copy-start.6 = (s32[2]{0:T(128)S(1)}, s32[2]{0:T(128)}, u32[]{:S(2)}) copy-start(s32[2]{0:T(128)} %constant.870.clone.1) | copy-start | bytes 28
  7.2 64.6 %all-gather.2.cloned.1.call-start = ((), (), s32[]{:S(2)}) async-start(), calls=%async_computation | async-start | bytes 8912896 | tf_op jit(solution)/shard_map/all_gather | solution.py:56
  11.5 333.5 %all-reduce.3.cloned.1.call-start = ((), (), s32[]{:S(2)}) async-start(), calls=%async_computation.1 | async-start | bytes 1048576 | tf_op jit(solution)/shard_map/psum | solution.py:72
  13.6 157.0 %copy-start.5 = (f32[33,1]{0,1:T(1,128)S(1)}, f32[33,1]{0,1:T(1,128)}, u32[]{:S(2)}) copy-start(f32[33,1]{0,1:T(1,128)} %constant.873.clone.1) | copy-start | bytes 400
  13.6 158.4 %copy-start.4 = (f32[33]{0:T(128)S(1)}, f32[33]{0:T(128)}, u32[]{:S(2)}) copy-start(f32[33]{0:T(128)} %constant.862.clone.1) | copy-start | bytes 400
  13.7 223.2 %copy-start.2 = (f32[1,131072]{1,0:T(1,128)S(1)}, f32[1,131072]{1,0:T(1,128)}, u32[]{:S(2)}) copy-start(f32[1,131072]{1,0:T(1,128)} %param.77) | copy-start | bytes 1572868
  13.7 223.2 %copy-start.3 = (f32[1,131072]{1,0:T(1,128)S(1)}, f32[1,131072]{1,0:T(1,128)}, u32[]{:S(2)}) copy-start(f32[1,131072]{1,0:T(1,128)} %param.78) | copy-start | bytes 1572868
  15.9 329.1 %copy-start.1 = (f32[131072]{0:T(1024)S(1)}, f32[131072]{0:T(1024)}, u32[]{:S(2)}) copy-start(f32[131072]{0:T(1024)} %param.79) | copy-start | bytes 1572868
  167.3 4.8 %copy-start = (f32[33,33]{0,1:T(8,128)}, f32[33,33]{0,1:T(8,128)S(1)}, u32[]{:S(2)}) copy-start(f32[33,33]{0,1:T(8,128)S(1)} %psum.14) | copy-start | bytes 13072
Sparse Core Ops, SparseCore 0:
  11.6 60.1 all-gather.1
  239.7 105.3 all-reduce.2
where the time goes:
time: 356 us; the launch traced here: 354 us
  waiting for transfers between devices  158 us (44%)
  blocking collectives  76.7 us (22%)
  other arithmetic  48.9 us (14%)
  between operations  47.4 us (13%)
  matrix products  14.4 us (4%)
  local copies, waits for them, and re-layouts  9.14 us (3%)
    psum x1, waiting for transfers between devices, shards(): summed = lax.psum(partial_sum, 'slot')  104 us
    psum x1, blocking collectives, shards(): gram_matrix = lax.psum(matrix, ('slot', 'param'))  76.7 us
    all_gather x1, waiting for transfers between devices, shards(): lax.all_gather(own_slabs, 'slot', axis=1, tiled=True)  53.7 us
    reduce_sum x16, other arithmetic, coefficients(): alpha_term = inverse * jnp.sum(coeffs * gram_matrix[:, position])  20.8 us
    dot_general x1, matrix products, pair_block(): jnp.einsum('akp,bjp->akbj', left, right, preferred_element_type=jnp.float32)  12.2 us
    reduce_sum x16, other arithmetic, coefficients(): jnp.sum(coeffs * gram_matrix[history + position, :])  9.68 us
  transfers between devices with their start and end apart: 2, of which 2 were waited for; matrix products, arithmetic and copies ran while one was open for 2% of the time, Pallas kernels for 0%

commit v1 on v0

v1 whole, which is shorter than its diff:
```python
import functools

import jax
import jax.numpy as jnp
from jax import lax
from jax.experimental import pallas as pl
from jax.experimental.pallas import tpu as pltpu
from jax.sharding import PartitionSpec as P

HIST = 16
SLOTS = 16
COLS = 16
ROWS = 1024
PIECE = ROWS // SLOTS
VECS = 40
LANES = 128
STRIDE = PIECE
F32, BF16 = jnp.float32, jnp.bfloat16
MESH = pl.DeviceIdType.MESH
STARTS = (0, 40, 72, 96, 112)


def lanes_between(low, high):
    lane = lax.broadcasted_iota(jnp.int32, (8, LANES), 1)
    return jnp.logical_and(lane >= low, lane < high)


def pack(matrix):
    packed = jnp.zeros((8, LANES), F32)
    for block in range(5):
        rows = matrix[8 * block : 8 * block + 8, :]
        shift = STARTS[block] - 8 * block
        if shift:
            rows = pltpu.roll(rows, shift, 1)
        packed = jnp.where(lanes_between(STARTS[block], STARTS[block] + 40 - 8 * block), rows, packed)
    return packed


def unpack(packed):
    blocks = []
    for block in range(5):
        shift = STARTS[block] - 8 * block
        rows = pltpu.roll(packed, LANES - shift, 1) if shift else packed
        blocks.append(jnp.where(lanes_between(8 * block, 40), rows, 0.0))
    upper = jnp.concatenate(blocks, axis=0)
    lower = jnp.transpose(upper)[:VECS, :]
    lower = jnp.concatenate([lower, jnp.zeros((VECS, LANES - VECS), F32)], axis=1)
    row = lax.broadcasted_iota(jnp.int32, (VECS, LANES), 0)
    col = lax.broadcasted_iota(jnp.int32, (VECS, LANES), 1)
    return jnp.where(col // 8 >= row // 8, upper, lower)


def recursion(gram):
    row = lax.broadcasted_iota(jnp.int32, (VECS, LANES), 0)
    col = lax.broadcasted_iota(jnp.int32, (VECS, LANES), 1)

    def column(j):
        return jnp.broadcast_to(gram[:, j : j + 1], (VECS, LANES))

    def spread(value, i):
        return jnp.broadcast_to(value[i : i + 1, :], (8, LANES))

    def tall(tile):
        return jnp.concatenate([tile] * (VECS // 8), axis=0)

    pairs = jnp.sum(jnp.where(col == row + HIST, gram, 0.0), axis=1, keepdims=True)
    inverses = 1.0 / jnp.broadcast_to(pairs, (VECS, LANES))
    inverse = [spread(inverses, i) for i in range(HIST)]
    products = -column(2 * HIST)
    alphas, steps, diffs = [None] * HIST, [None] * HIST, [None] * HIST
    for i in reversed(range(HIST)):
        alphas[i] = inverse[i] * spread(products, i)
        products = products - tall(alphas[i]) * column(HIST + i)
    scale = spread(column(2 * HIST - 1), HIST - 1) / spread(column(2 * HIST - 1), 2 * HIST - 1)
    products = products * tall(scale)
    for i in range(HIST):
        steps[i] = alphas[i] - inverse[i] * spread(products, HIST + i)
        products = products + tall(steps[i]) * column(i)
        diffs[i] = -alphas[i] * scale
    return steps, diffs, -scale


def kernel(
    step_hbm, diff_hbm, grad_hbm, out_ref, gram_ref,
    step_v, diff_v, grad_v, hi_send, lo_send, hi_recv, lo_recv, wide, square, part, slot_parts, col_parts,
    load_sem, hi_ss, hi_rs, lo_ss, lo_rs, slot_ss, slot_rs, col_ss, col_rs, dir_ss, dir_rs, sib_ss, sib_rs,
):
    me = lax.axis_index("slot")
    col = lax.axis_index("param")
    mate = me + 1 - 2 * lax.rem(me, 2)
    own_rows = pl.ds(pl.multiple_of(me * PIECE, PIECE), PIECE)

    loads = [
        pltpu.make_async_copy(step_hbm, step_v, load_sem.at[0]),
        pltpu.make_async_copy(diff_hbm, diff_v, load_sem.at[1]),
        pltpu.make_async_copy(grad_hbm.at[own_rows], grad_v, load_sem.at[2]),
    ]
    for load in loads:
        load.start()

    barrier = pltpu.get_barrier_semaphore()
    for d in range(1, SLOTS):
        pl.semaphore_signal(barrier, inc=1, device_id={"slot": lax.rem(me + d, SLOTS)}, device_id_type=MESH)
    for d in range(1, COLS):
        pl.semaphore_signal(barrier, inc=1, device_id={"param": lax.rem(col + d, COLS)}, device_id_type=MESH)
    for load in loads:
        load.wait()
    pl.semaphore_wait(barrier, SLOTS + COLS - 2)

    def halves(dest):
        rows = pl.ds(pl.multiple_of(dest * PIECE, PIECE), PIECE)
        return step_v[rows, :], diff_v[rows, :]

    hi_copies = []
    for d in range(1, SLOTS):
        dest = lax.rem(me + d, SLOTS)
        s, y = halves(dest)
        hi_send[dest, :PIECE, :] = s.astype(BF16)
        hi_send[dest, PIECE:, :] = y.astype(BF16)
        copy = pltpu.make_async_remote_copy(
            hi_send.at[dest], hi_recv.at[me], hi_ss.at[d], hi_rs.at[d], device_id={"slot": dest}, device_id_type=MESH
        )
        copy.start()
        hi_copies.append(copy)
    s, y = halves(me)
    hi_recv[me, :PIECE, :] = s.astype(BF16)
    hi_recv[me, PIECE:, :] = y.astype(BF16)

    for k in range(SLOTS):
        for half, source in ((0, step_v), (PIECE, diff_v)):
            v = source[k * PIECE : (k + 1) * PIECE, :]
            lo_send[k, half : half + PIECE, :] = (v - v.astype(BF16).astype(F32)).astype(BF16)
    lo_recv[me] = lo_send[me]

    wide[2 * HIST * STRIDE : 2 * HIST * STRIDE + PIECE, :] = grad_v[...].astype(BF16).astype(F32)
    for j in range(2 * HIST + 1, VECS):
        wide[j * STRIDE : j * STRIDE + PIECE, :] = jnp.zeros((PIECE, LANES), F32)

    for copy in hi_copies:
        copy.wait_recv()

    for k in range(SLOTS):
        wide[k * STRIDE : k * STRIDE + PIECE, :] = hi_recv[k, :PIECE, :].astype(F32)
        wide[(HIST + k) * STRIDE : (HIST + k) * STRIDE + PIECE, :] = hi_recv[k, PIECE:, :].astype(F32)
    rows = [wide[pl.ds(r, VECS, stride=STRIDE), :].astype(BF16) for r in range(PIECE)]
    flat = jnp.concatenate(rows, axis=1)
    square[...] = jnp.zeros((VECS, LANES), F32)
    square[:, :VECS] = lax.dot_general(flat, flat, (((1,), (1,)), ((), ())), preferred_element_type=F32)
    packed = pack(square[...])
    part[0] = packed
    slot_parts[me] = packed
    slot_copies = []
    for d in range(1, SLOTS):
        dest = lax.rem(me + d, SLOTS)
        copy = pltpu.make_async_remote_copy(
            part.at[0], slot_parts.at[me], slot_ss.at[d], slot_rs.at[d], device_id={"slot": dest}, device_id_type=MESH
        )
        copy.start()
        slot_copies.append(copy)

    lo_copies = []
    for d in range(1, SLOTS):
        dest = lax.rem(me + d, SLOTS)
        copy = pltpu.make_async_remote_copy(
            lo_send.at[dest], lo_recv.at[me], lo_ss.at[d], lo_rs.at[d], device_id={"slot": dest}, device_id_type=MESH
        )
        copy.start()
        lo_copies.append(copy)

    for copy in slot_copies:
        copy.wait_recv()
    total = slot_parts[0]
    for k in range(1, SLOTS):
        total = total + slot_parts[k]
    part[1] = total
    col_parts[col] = total
    col_copies = []
    for d in range(1, COLS):
        dest = lax.rem(col + d, COLS)
        copy = pltpu.make_async_remote_copy(
            part.at[1], col_parts.at[col], col_ss.at[d], col_rs.at[d], device_id={"param": dest}, device_id_type=MESH
        )
        copy.start()
        col_copies.append(copy)
    for copy in col_copies:
        copy.wait_recv()
    total = col_parts[0]
    for k in range(1, COLS):
        total = total + col_parts[k]
    gram = unpack(total * (1.0 / (ROWS * LANES * COLS)))
    gram_ref[...] = gram[: 2 * HIST + 1, : 2 * HIST + 1]
    steps, diffs, grad_coeff = recursion(gram)

    for copy in lo_copies:
        copy.wait_recv()
    for t in range(PIECE // 8):
        low, high = 8 * t, 8 * t + 8
        acc = grad_coeff * grad_v[low:high, :]
        for k in range(SLOTS):
            s = hi_recv[k, low:high, :].astype(F32) + lo_recv[k, low:high, :].astype(F32)
            y = hi_recv[k, PIECE + low : PIECE + high, :].astype(F32) + lo_recv[k, PIECE + low : PIECE + high, :].astype(F32)
            acc = acc + steps[k] * s + diffs[k] * y
        out_ref[pl.ds(pl.multiple_of(me * PIECE + low, 8), 8), :] = acc

    chips = SLOTS // 2

    def piece(slot):
        return out_ref.at[pl.ds(pl.multiple_of(slot * PIECE, PIECE), PIECE)]

    dir_copies = {}
    for d in (4, 3, 5, 2, 6, 1, 7):
        dest = lax.rem(me + 2 * d, SLOTS)
        copy = pltpu.make_async_remote_copy(
            piece(me), piece(me), dir_ss.at[d], dir_rs.at[d], device_id={"slot": dest}, device_id_type=MESH
        )
        copy.start()
        dir_copies[d] = copy
    sib_copies = []
    for d in (0, 1, 7, 2, 6, 3, 5, 4):
        if d:
            dir_copies[d].wait_recv()
        source = lax.rem(me + 2 * (chips - d), SLOTS)
        copy = pltpu.make_async_remote_copy(
            piece(source), piece(source), sib_ss.at[d], sib_rs.at[d], device_id={"slot": mate}, device_id_type=MESH
        )
        copy.start()
        sib_copies.append(copy)
    for copy in sib_copies:
        copy.wait_recv()
    for copy in hi_copies + slot_copies + lo_copies + col_copies + list(dir_copies.values()) + sib_copies:
        copy.wait_send()


def call(step, diff, grad):
    dma = pltpu.SemaphoreType.DMA
    return pl.pallas_call(
        kernel,
        out_shape=(
            jax.ShapeDtypeStruct((ROWS, LANES), F32),
            jax.ShapeDtypeStruct((2 * HIST + 1, 2 * HIST + 1), F32),
        ),
        in_specs=[pl.BlockSpec(memory_space=pl.ANY)] * 3,
        out_specs=(pl.BlockSpec(memory_space=pltpu.VMEM), pl.BlockSpec(memory_space=pltpu.VMEM)),
        scratch_shapes=[
            pltpu.VMEM((ROWS, LANES), F32),
            pltpu.VMEM((ROWS, LANES), F32),
            pltpu.VMEM((PIECE, LANES), F32),
            pltpu.VMEM((SLOTS, 2 * PIECE, LANES), BF16),
            pltpu.VMEM((SLOTS, 2 * PIECE, LANES), BF16),
            pltpu.VMEM((SLOTS, 2 * PIECE, LANES), BF16),
            pltpu.VMEM((SLOTS, 2 * PIECE, LANES), BF16),
            pltpu.VMEM((VECS * STRIDE, LANES), F32),
            pltpu.VMEM((VECS, LANES), F32),
            pltpu.VMEM((2, 8, LANES), F32),
            pltpu.VMEM((SLOTS, 8, LANES), F32),
            pltpu.VMEM((COLS, 8, LANES), F32),
            dma((3,)),
            *[dma((SLOTS,))] * 8,
            *[dma((SLOTS // 2,))] * 4,
        ],
        compiler_params=pltpu.CompilerParams(
            collective_id=0, has_side_effects=True, vmem_limit_bytes=60 * 2**20
        ),
        name="lbfgs",
    )(step, diff, grad)


def shards(step_hist, diff_hist, gradient):
    shape = (ROWS, LANES)
    direction, gram = call(step_hist.reshape(shape), diff_hist.reshape(shape), gradient.reshape(shape))
    return direction.reshape(ROWS * LANES), gram


def solution(mesh):
    in_specs = (P("slot", "param"), P("slot", "param"), P("param"))
    out_specs = (P("param"), P())
    return jax.shard_map(shards, mesh=mesh, in_specs=in_specs, out_specs=out_specs, check_vma=False)
```

time: 356 us -> 56.1 us (0.16)
  waiting for transfers between devices: 158 us -> 0 us
  blocking collectives: 76.7 us -> 0 us
  Pallas kernels: 0 us -> 52.9 us
  other arithmetic: 48.9 us -> 0 us
  between operations: 47.4 us -> 0.65 us
  matrix products: 14.4 us -> 0 us
  local copies, waits for them, and re-layouts: 9.14 us -> 2.48 us
    psum x1 -> x0, waiting for transfers between devices: 104 us -> none  [shards(): summed = lax.psum(partial_sum, 'slot')]
    psum x1 -> x0, blocking collectives: 76.7 us -> none  [shards(): gram_matrix = lax.psum(matrix, ('slot', 'param'))]
    all_gather x1 -> x0, waiting for transfers between devices: 53.7 us -> none  [shards(): lax.all_gather(own_slabs, 'slot', axis=1, tiled=True)]
    pallas_call x0 -> x1, Pallas kernels: none -> 52.9 us  [call(): pl.pallas_call(kernel, out_shape=(jax.ShapeDtypeStruct((ROWS, LANES), F32...]
    reduce_sum x32 -> x0, other arithmetic: 30.5 us -> none  [the longest x16 20.8 us: coefficients(): alpha_term = inverse * jnp.sum(coeffs * gram_matrix[:, position])]
    dot_general x2 -> x0, matrix products: 14.4 us -> none  [the longest x1 12.2 us: pair_block(): jnp.einsum('akp,bjp->akbj', left, right, preferred_element_type=jnp.float32)]
    another operation x5 -> x0, other arithmetic: 6.83 us -> none
    add x2 -> x0, other arithmetic: 5.19 us -> none  [the longest x1 2.67 us: shards(): partial_sum + jnp.dot(diff_coeffs, diff_hist, precision=lax.Precision.HIG...]
  transfers between devices with their start and end apart: 2 -> 0, of which waited for: 2 -> 0; matrix products, arithmetic and copies ran while one was open for 2% -> 0% of each run, Pallas kernels for 0% -> 0%
where the time goes in v1:
time: 56.1 us; the launch traced here: 56 us
  Pallas kernels  52.9 us (94%)
  local copies, waits for them, and re-layouts  2.48 us (4%)
  between operations  0.65 us (1%)
    pallas_call x1, Pallas kernels, call(): pl.pallas_call(kernel, out_shape=(jax.ShapeDtypeStruct((ROWS, LANES), F32...  52.9 us
    unnamed x4, local copies, waits for them, and re-layouts  2.48 us

profile of v1, /device:TPU:1, one launch (start us, length us, event | category | flops | bytes accessed | tf_op | source)
XLA Modules:
  0.0 56.0 jit_solution(9793450749227939360)
XLA Ops:
  0.6 52.9 %lbfgs.1 = (f32[1024,128]{1,0:T(8,128)}, f32[33,33]{1,0:T(8,128)}) custom-call(f32[1024,128]{1,0:T(8,128)} %bitcast.4, f32[1024,128]{1,0:T(8,128)} %bitcast.5, f32[1024,128]{1,0:T(8,128)} %bitcast.6), custom_call_target="tpu_custom_call" | custom-call | tf_op jit(solution)/shard_map/lbfgs/pallas_call | solution.py:236
  53.5 0.0 copy-start
  53.5 1.9 %copy.7 = f32[131072]{0:T(1024)} copy(f32[131072]{0:T(1024)} %bitcast.7) | data formatting | bytes 1048576
  55.4 0.0 copy-done
  55.4 0.6 %copy.8 = f32[33,33]{1,0:T(8,128)} copy(f32[33,33]{1,0:T(8,128)S(1)} %copy-done) | data formatting | bytes 8712
Async XLA Ops:
  53.5 1.9 %copy-start = (f32[33,33]{1,0:T(8,128)S(1)}, f32[33,33]{1,0:T(8,128)}, u32[]{:S(2)}) copy-start(f32[33,33]{1,0:T(8,128)} %get-tuple-element.9) | copy-start | bytes 13072

commit v2 on v1

v2 whole, which is shorter than its diff:
```python
import functools

import jax
import jax.numpy as jnp
from jax import lax
from jax.experimental import pallas as pl
from jax.experimental.pallas import tpu as pltpu
from jax.sharding import PartitionSpec as P

HIST = 16
SLOTS = 16
COLS = 16
ROWS = 1024
PIECE = ROWS // SLOTS
VECS = 40
LANES = 128
STRIDE = 72
F32, BF16 = jnp.float32, jnp.bfloat16
MESH = pl.DeviceIdType.MESH
SIDE = 4
CHIPS = SLOTS // 2
VMEM_LIMIT = 56 * 2**20
HI_DRAIN = True
LOADS_FIRST = 4
RING_FIRST = True
CORES_IN_PLANE = False
TILE = 16
HI_PARTS = 1
SPAN = PIECE // HI_PARTS
CUTS = (0, 16, 64)
LO_EARLY = 1
PARTS = len(CUTS) - 1
HOPS = (4, 3, 5, 2, 6, 1, 7, 0)
RING = [(dz, flip) for dz in HOPS for flip in (0, 1) if dz or flip]
RING_SUM = [(dz, flip) for dz, flip in RING if not (CORES_IN_PLANE and (flip or not dz))]
NEAR = ()
PASSED = (4, 3, 5, 2, 6, 1, 7)
SPREAD = [(dz, flip) for dz in HOPS for flip in (0, 1) if (not flip and dz) or (flip and (dz in NEAR or not dz))]
PASS = [dz for dz in PASSED if dz not in NEAR]
PLANE = sorted(
    ((x, y, flip) for x in range(SIDE) for y in range(SIDE) for flip in range(1 + CORES_IN_PLANE) if x or y or flip),
    key=lambda o: (-min(o[0], SIDE - o[0]) - min(o[1], SIDE - o[1]), o),
)
STARTS = (0, 40, 72, 96, 112)


def lanes_between(low, high):
    lane = lax.broadcasted_iota(jnp.int32, (8, LANES), 1)
    return jnp.logical_and(lane >= low, lane < high)


def pack(matrix):
    packed = jnp.zeros((8, LANES), F32)
    for block in range(5):
        rows = matrix[8 * block : 8 * block + 8, :]
        shift = STARTS[block] - 8 * block
        if shift:
            rows = pltpu.roll(rows, shift, 1)
        packed = jnp.where(lanes_between(STARTS[block], STARTS[block] + 40 - 8 * block), rows, packed)
    return packed


def unpack(packed):
    blocks = []
    for block in range(5):
        shift = STARTS[block] - 8 * block
        rows = pltpu.roll(packed, LANES - shift, 1) if shift else packed
        blocks.append(jnp.where(lanes_between(8 * block, 40), rows, 0.0))
    upper = jnp.concatenate(blocks, axis=0)
    lower = jnp.transpose(upper)[:VECS, :]
    lower = jnp.concatenate([lower, jnp.zeros((VECS, LANES - VECS), F32)], axis=1)
    row = lax.broadcasted_iota(jnp.int32, (VECS, LANES), 0)
    col = lax.broadcasted_iota(jnp.int32, (VECS, LANES), 1)
    return jnp.where(col // 8 >= row // 8, upper, lower)


def recursion(gram):
    row = lax.broadcasted_iota(jnp.int32, (VECS, LANES), 0)
    col = lax.broadcasted_iota(jnp.int32, (VECS, LANES), 1)

    def column(j):
        return jnp.broadcast_to(gram[:, j : j + 1], (VECS, LANES))

    def spread(value, i):
        return jnp.broadcast_to(value[i : i + 1, :], (8, LANES))

    def tall(tile):
        return jnp.concatenate([tile] * (VECS // 8), axis=0)

    pairs = jnp.sum(jnp.where(col == row + HIST, gram, 0.0), axis=1, keepdims=True)
    inverses = 1.0 / jnp.broadcast_to(pairs, (VECS, LANES))
    inverse = [spread(inverses, i) for i in range(HIST)]
    products = -column(2 * HIST)
    alphas, steps, diffs = [None] * HIST, [None] * HIST, [None] * HIST
    for i in reversed(range(HIST)):
        alphas[i] = inverse[i] * spread(products, i)
        products = products - tall(alphas[i]) * column(HIST + i)
    scale = spread(column(2 * HIST - 1), HIST - 1) / spread(column(2 * HIST - 1), 2 * HIST - 1)
    products = products * tall(scale)
    for i in range(HIST):
        steps[i] = alphas[i] - inverse[i] * spread(products, HIST + i)
        products = products + tall(steps[i]) * column(i)
        diffs[i] = -alphas[i] * scale
    return steps, diffs, -scale


class Net:
    def __init__(self):
        self.sent, self.open, self.local = [], [], []

    def send(self, source, target, send_sem, recv_sem, **peer):
        copy = pltpu.make_async_remote_copy(
            source, target, send_sem, recv_sem, device_id=peer, device_id_type=MESH
        )
        copy.start()
        self.sent.append(copy)
        self.open.append(copy)
        return copy

    def receive(self, *copies):
        for copy in copies:
            copy.wait_recv()
            self.open = [c for c in self.open if c is not copy]

    def drain(self, *copies):
        for copy in copies:
            copy.wait_send()
            self.sent = [c for c in self.sent if c is not copy]

    def finish(self):
        for copy in self.local:
            copy.wait()
        self.receive(*list(self.open))
        self.drain(*list(self.sent))


def kernel(
    step_hbm, diff_hbm, grad_hbm, out_ref, gram_ref,
    step_v, diff_v, grad_v, hi_send, lo_send, hi_recv, lo_recv, wide, square, staged, plane_parts, ring_parts,
    load_sem, grad_sem, hi_ss, hi_rs, lo_ss, lo_rs, plane_ss, plane_rs, ring_ss, ring_rs, dir_ss, dir_rs, pass_ss, pass_rs,
):
    net = Net()
    me = lax.axis_index("slot")
    col = lax.axis_index("param")
    mate = me + 1 - 2 * lax.rem(me, 2)
    chip, core = me // 2, lax.rem(me, 2)
    own_rows = pl.ds(pl.multiple_of(me * PIECE, PIECE), PIECE)

    def across(dx, dy, flip):
        x, y = col // SIDE, lax.rem(col, SIDE)
        peer = {"param": lax.rem(x + dx, SIDE) * SIDE + lax.rem(y + dy, SIDE)}
        return {**peer, "slot": mate} if flip else peer

    def along(dz, flip):
        return lax.rem(chip + dz, CHIPS) * 2 + (1 - core if flip else core)

    def load(dz):
        rows = pl.ds(pl.multiple_of(lax.rem(chip + dz, CHIPS) * 2 * PIECE, 2 * PIECE), 2 * PIECE)
        return [
            pltpu.make_async_copy(source.at[rows], target.at[rows], load_sem.at[i, dz])
            for i, (source, target) in enumerate(((step_hbm, step_v), (diff_hbm, diff_v)))
        ]

    loads = {dz: load(dz) for dz in HOPS}
    net.local = [c for dz in HOPS for c in loads[dz]]
    grad_load = pltpu.make_async_copy(grad_hbm.at[own_rows], grad_v, grad_sem.at[0])
    for dz in HOPS[:LOADS_FIRST]:
        for copy in loads[dz]:
            copy.start()
    barrier = pltpu.get_barrier_semaphore()
    peers = [{"slot": along(*offset)} for offset in RING] + [across(*offset) for offset in PLANE]
    for peer in peers:
        pl.semaphore_signal(barrier, inc=1, device_id=peer, device_id_type=MESH)
    for dz in HOPS[LOADS_FIRST:]:
        for copy in loads[dz]:
            copy.start()
    grad_load.start()
    net.local.append(grad_load)
    pl.semaphore_wait(barrier, len(peers))
    hi_copies = []
    for part in range(HI_PARTS):
        rows = pl.ds(2 * SPAN * part, 2 * SPAN)
        for i, (dz, flip) in enumerate(RING):
            if not part and (not flip or not dz):
                for copy in loads[dz]:
                    copy.wait()
                    net.local = [c for c in net.local if c is not copy]
            dest = along(dz, flip)
            for half, source in ((0, step_v), (SPAN, diff_v)):
                v = source[pl.ds(pl.multiple_of(dest * PIECE + part * SPAN, 8), SPAN), :]
                at = 2 * SPAN * part + half
                hi_send[dest, at : at + SPAN, :] = v.astype(BF16)
            hi_copies.append(
                net.send(hi_send.at[dest, rows], hi_recv.at[me, rows], hi_ss.at[part, i], hi_rs.at[part, i], slot=dest)
            )
        for half, source in ((0, step_v), (SPAN, diff_v)):
            v = source[pl.ds(pl.multiple_of(me * PIECE + part * SPAN, 8), SPAN), :]
            at = 2 * SPAN * part + half
            hi_recv[me, at : at + SPAN, :] = v.astype(BF16)

    for k in range(SLOTS):
        for half, source in ((0, step_v), (TILE, diff_v)):
            for row in range(0, PIECE, TILE):
                v = source[k * PIECE + row : k * PIECE + row + TILE, :]
                lo_send[k, 2 * row + half : 2 * row + half + TILE, :] = (v - v.astype(BF16).astype(F32)).astype(BF16)

    def send_lo(part):
        rows = pl.ds(2 * CUTS[part], 2 * (CUTS[part + 1] - CUTS[part]))
        copies = []
        for i, offset in enumerate(RING):
            dest = along(*offset)
            copies.append(
                net.send(lo_send.at[dest, rows], lo_recv.at[me, rows], lo_ss.at[part, i], lo_rs.at[part, i], slot=dest)
            )
        return copies

    if HI_DRAIN:
        net.drain(*[c for c in hi_copies if any(c is o for o in net.sent)])
    lo_copies = [send_lo(part) for part in range(LO_EARLY)]
    lo_recv[me] = lo_send[me]
    grad_load.wait()
    net.local = []
    wide[2 * HIST * STRIDE : 2 * HIST * STRIDE + PIECE, :] = grad_v[...].astype(BF16).astype(F32)
    for j in range(2 * HIST + 1, VECS):
        wide[j * STRIDE : j * STRIDE + PIECE, :] = jnp.zeros((PIECE, LANES), F32)

    def widen(k, part):
        at = 2 * SPAN * part
        for j, row in ((k, at), (HIST + k, at + SPAN)):
            rows = pl.ds(pl.multiple_of(j * STRIDE + part * SPAN, 8), SPAN)
            wide[rows, :] = hi_recv[k, row : row + SPAN, :].astype(F32)

    products = jnp.zeros((VECS, VECS), F32)
    for part in range(HI_PARTS):
        widen(me, part)
        for i, (dz, flip) in enumerate(RING):
            net.receive(hi_copies[part * len(RING) + i])
            widen(along(CHIPS - dz, flip), part)
        rows = [wide[pl.ds(r, VECS, stride=STRIDE), :].astype(BF16) for r in range(part * SPAN, (part + 1) * SPAN)]
        flat = jnp.concatenate(rows, axis=1)
        products = products + lax.dot_general(flat, flat, (((1,), (1,)), ((), ())), preferred_element_type=F32)
    square[...] = jnp.zeros((VECS, LANES), F32)
    square[:, :VECS] = products
    packed = pack(square[...])

    def exchange(value, number, parts, mine, peers, send_sems, recv_sems):
        staged[number] = value
        parts[mine] = value
        return [
            net.send(staged.at[number], parts.at[mine], send_sems.at[i], recv_sems.at[i], **peer)
            for i, peer in enumerate(peers)
        ]

    def total(parts):
        values = [parts[k] for k in range(parts.shape[0])]
        while len(values) > 1:
            values = [a + b for a, b in zip(values[::2], values[1::2])]
        return values[0]

    plane_mine = col + COLS * core if CORES_IN_PLANE else col
    ring_mine = chip if CORES_IN_PLANE else me
    ring_peers = [{"slot": along(*offset)} for offset in RING_SUM]
    plane_peers = [across(*offset) for offset in PLANE]
    stages = [(ring_parts, ring_mine, ring_peers, ring_ss, ring_rs), (plane_parts, plane_mine, plane_peers, plane_ss, plane_rs)]
    if not RING_FIRST:
        stages.reverse()
    copies = exchange(packed, 0, *stages[0])
    if RING_FIRST:
        lo_copies += [send_lo(part) for part in range(LO_EARLY, PARTS)]
    net.receive(*reversed(copies))
    copies = exchange(total(stages[0][0]), 1, *stages[1])
    if not RING_FIRST:
        lo_copies += [send_lo(part) for part in range(LO_EARLY, PARTS)]
    net.receive(*reversed(copies))
    gram = unpack(total(stages[1][0]) * (1.0 / (ROWS * LANES * COLS)))
    gram_ref[...] = gram[: 2 * HIST + 1, : 2 * HIST + 1]
    steps, diffs, grad_coeff = recursion(gram)

    def piece(slot, part):
        start = pl.multiple_of(slot * PIECE + CUTS[part], 8)
        return out_ref.at[pl.ds(start, CUTS[part + 1] - CUTS[part])]

    dir_copies = {}
    for n in range(PARTS):
        net.receive(*lo_copies[n])
        for low in range(CUTS[n], CUTS[n + 1], 8):
            acc = grad_coeff * grad_v[low : low + 8, :]
            at = low // TILE * 2 * TILE + low % TILE
            up = low // SPAN * 2 * SPAN + low % SPAN
            for k in range(SLOTS):
                s = hi_recv[k, up : up + 8, :].astype(F32) + lo_recv[k, at : at + 8, :].astype(F32)
                y = hi_recv[k, up + SPAN : up + SPAN + 8, :].astype(F32)
                y = y + lo_recv[k, at + TILE : at + TILE + 8, :].astype(F32)
                acc = acc + steps[k] * s + diffs[k] * y
            out_ref[pl.ds(pl.multiple_of(me * PIECE + low, 8), 8), :] = acc
        for i, (dz, flip) in enumerate(SPREAD):
            dir_copies[n, dz, flip] = net.send(
                piece(me, n), piece(me, n), dir_ss.at[n, i], dir_rs.at[n, i], slot=along(dz, flip)
            )
    for n in range(PARTS):
        for dz in PASS:
            net.receive(dir_copies[n, dz, 0])
            source = along(CHIPS - dz, 0)
            net.send(piece(source, n), piece(source, n), pass_ss.at[n, dz], pass_rs.at[n, dz], slot=mate)
    net.finish()


def call(step, diff, grad):
    dma = pltpu.SemaphoreType.DMA
    return pl.pallas_call(
        kernel,
        out_shape=(pltpu.VMEM((ROWS, LANES), F32), pltpu.VMEM((2 * HIST + 1, 2 * HIST + 1), F32)),
        in_specs=[pl.BlockSpec(memory_space=pltpu.HBM)] * 3,
        out_specs=(pl.BlockSpec(memory_space=pltpu.VMEM), pl.BlockSpec(memory_space=pltpu.VMEM)),
        scratch_shapes=[
            pltpu.VMEM((ROWS, LANES), F32),
            pltpu.VMEM((ROWS, LANES), F32),
            pltpu.VMEM((PIECE, LANES), F32),
            pltpu.VMEM((SLOTS, 2 * PIECE, LANES), BF16),
            pltpu.VMEM((SLOTS, 2 * PIECE, LANES), BF16),
            pltpu.VMEM((SLOTS, 2 * PIECE, LANES), BF16),
            pltpu.VMEM((SLOTS, 2 * PIECE, LANES), BF16),
            pltpu.VMEM((VECS * STRIDE, LANES), F32),
            pltpu.VMEM((VECS, LANES), F32),
            pltpu.VMEM((2, 8, LANES), F32),
            pltpu.VMEM((len(PLANE) + 1, 8, LANES), F32),
            pltpu.VMEM((len(RING_SUM) + 1, 8, LANES), F32),
            dma((2, CHIPS)),
            dma((1,)),
            *[dma((HI_PARTS, SLOTS))] * 2,
            *[dma((PARTS, SLOTS))] * 2,
            *[dma((len(PLANE),))] * 2,
            *[dma((len(RING_SUM),))] * 2,
            *[dma((PARTS, len(SPREAD)))] * 2,
            *[dma((PARTS, CHIPS))] * 2,
        ],
        compiler_params=pltpu.CompilerParams(
            collective_id=0, has_side_effects=True, vmem_limit_bytes=VMEM_LIMIT
        ),
        name="lbfgs",
    )(step, diff, grad)


def write(direction_v, gram_v, direction_hbm, gram_hbm, sem):
    copies = [
        pltpu.make_async_copy(direction_v, direction_hbm, sem.at[0]),
        pltpu.make_async_copy(gram_v, gram_hbm, sem.at[1]),
    ]
    for copy in copies:
        copy.start()
    for copy in copies:
        copy.wait()


def store(direction, gram):
    return pl.pallas_call(
        write,
        out_shape=(
            jax.ShapeDtypeStruct(direction.shape, F32),
            jax.ShapeDtypeStruct(gram.shape, F32),
        ),
        in_specs=[pl.BlockSpec(memory_space=pltpu.VMEM)] * 2,
        out_specs=(pl.BlockSpec(memory_space=pl.ANY), pl.BlockSpec(memory_space=pl.ANY)),
        scratch_shapes=[pltpu.SemaphoreType.DMA((2,))],
        compiler_params=pltpu.CompilerParams(vmem_limit_bytes=2**20),
        name="store",
    )(direction, gram)


def shards(step_hist, diff_hist, gradient):
    shape = (ROWS, LANES)
    direction, gram = store(*call(step_hist.reshape(shape), diff_hist.reshape(shape), gradient.reshape(shape)))
    return direction.reshape(ROWS * LANES), gram


def solution(mesh):
    in_specs = (P("slot", "param"), P("slot", "param"), P("param"))
    out_specs = (P("param"), P())
    return jax.shard_map(shards, mesh=mesh, in_specs=in_specs, out_specs=out_specs, check_vma=False)
```

time: 56.1 us -> 48.9 us (0.87)
  Pallas kernels: 52.9 us -> 48.2 us
  local copies, waits for them, and re-layouts: 2.48 us -> 0 us
    pallas_call x1 -> x2, Pallas kernels: 52.9 us -> 48.2 us  [the longest x1 47.4 us: call(): pl.pallas_call(kernel, out_shape=(pltpu.VMEM((ROWS, LANES), F32), pltpu.V...]
    unnamed x4 -> x0, local copies, waits for them, and re-layouts: 2.48 us -> none
where the time goes in v2:
time: 48.9 us; the launch traced here: 48.8 us
  Pallas kernels  48.2 us (99%)
  between operations  0.64 us (1%)
    pallas_call x1, Pallas kernels, call(): pl.pallas_call(kernel, out_shape=(pltpu.VMEM((ROWS, LANES), F32), pltpu.V...  47.4 us

profile of v2, /device:TPU:1, one launch (start us, length us, event | category | flops | bytes accessed | tf_op | source)
XLA Modules:
  0.0 48.8 jit_solution(1402811764350128870)
XLA Ops:
  0.6 47.4 %lbfgs.1 = (f32[1024,128]{1,0:T(8,128)S(1)}, f32[33,33]{1,0:T(8,128)S(1)}) custom-call(f32[1024,128]{1,0:T(8,128)} %bitcast.4, f32[1024,128]{1,0:T(8,128)} %bitcast.5, f32[1024,128]{1,0:T(8,128)} %bitcast.6), custom_call_target="tpu_custom_call" | custom-call | tf_op jit(solution)/shard_map/lbfgs/pallas_call | solution.py:310
  48.0 0.8 %store.1 = (f32[1024,128]{1,0:T(8,128)}, f32[33,33]{1,0:T(8,128)}) custom-call(f32[1024,128]{1,0:T(8,128)S(1)} %get-tuple-element.6.direction_v, f32[33,33]{1,0:T(8,128)S(1)} %get-tuple-element.7.gram_v), custom_call_target="tpu_custom_call" | custom-call | tf_op jit(solution)/shard_map/store/pallas_call | solution.py:356

commit v3 on v2

--- a/solution.py
+++ b/solution.py
@@ -14,14 +14,17 @@
 PIECE = ROWS // SLOTS
 VECS = 40
 LANES = 128
-STRIDE = 72
+STRIDE = PIECE + 8
 F32, BF16 = jnp.float32, jnp.bfloat16
 MESH = pl.DeviceIdType.MESH
 SIDE = 4
 CHIPS = SLOTS // 2
+MERGED = True
+EARLY_DRAIN = True
+HI_AHEAD = True
 VMEM_LIMIT = 56 * 2**20
 HI_DRAIN = True
-LOADS_FIRST = 4
+LOADS_FIRST = 0
 RING_FIRST = True
 CORES_IN_PLANE = False
 TILE = 16
@@ -30,16 +33,20 @@
 CUTS = (0, 16, 64)
 LO_EARLY = 1
 PARTS = len(CUTS) - 1
+
+
+def hops(offset, around):
+    return min(offset, around - offset)
+
+
 HOPS = (4, 3, 5, 2, 6, 1, 7, 0)
 RING = [(dz, flip) for dz in HOPS for flip in (0, 1) if dz or flip]
 RING_SUM = [(dz, flip) for dz, flip in RING if not (CORES_IN_PLANE and (flip or not dz))]
-NEAR = ()
-PASSED = (4, 3, 5, 2, 6, 1, 7)
-SPREAD = [(dz, flip) for dz in HOPS for flip in (0, 1) if (not flip and dz) or (flip and (dz in NEAR or not dz))]
-PASS = [dz for dz in PASSED if dz not in NEAR]
+ORDER = (0, 4, 1, 5, 2, 6, 3, 7)
+PASS = (4, 3, 5, 2, 6, 1, 7)
 PLANE = sorted(
     ((x, y, flip) for x in range(SIDE) for y in range(SIDE) for flip in range(1 + CORES_IN_PLANE) if x or y or flip),
-    key=lambda o: (-min(o[0], SIDE - o[0]) - min(o[1], SIDE - o[1]), o),
+    key=lambda o: (-hops(o[0], SIDE) - hops(o[1], SIDE), o),
 )
 STARTS = (0, 40, 72, 96, 112)
 
@@ -168,7 +175,9 @@
         for copy in loads[dz]:
             copy.start()
     barrier = pltpu.get_barrier_semaphore()
-    peers = [{"slot": along(*offset)} for offset in RING] + [across(*offset) for offset in PLANE]
+    peers = [(hops(dz, CHIPS), {"slot": along(dz, flip)}) for dz, flip in RING]
+    peers += [(hops(dx, SIDE) + hops(dy, SIDE), across(dx, dy, flip)) for dx, dy, flip in PLANE]
+    peers = [peer for _, peer in sorted(peers, key=lambda p: -p[0])] if MERGED else [peer for _, peer in peers]
     for peer in peers:
         pl.semaphore_signal(barrier, inc=1, device_id=peer, device_id_type=MESH)
     for dz in HOPS[LOADS_FIRST:]:
@@ -268,7 +277,10 @@
     if RING_FIRST:
         lo_copies += [send_lo(part) for part in range(LO_EARLY, PARTS)]
     net.receive(*reversed(copies))
+    first = copies
     copies = exchange(total(stages[0][0]), 1, *stages[1])
+    if EARLY_DRAIN:
+        net.drain(*first)
     if not RING_FIRST:
         lo_copies += [send_lo(part) for part in range(LO_EARLY, PARTS)]
     net.receive(*reversed(copies))
@@ -280,28 +292,54 @@
         start = pl.multiple_of(slot * PIECE + CUTS[part], 8)
         return out_ref.at[pl.ds(start, CUTS[part + 1] - CUTS[part])]
 
-    dir_copies = {}
+    def combine(row, at, coeffs, source, span, acc):
+        for k in range(SLOTS):
+            acc = acc + coeffs[0][k] * source[k, at : at + 8, :].astype(F32)
+            acc = acc + coeffs[1][k] * source[k, at + span : at + span + 8, :].astype(F32)
+        return acc
+
+    def each(k, n, step):
+        copy = pltpu.make_async_remote_copy(
+            piece(me, n), piece(me, n), dir_ss.at[n, k], dir_rs.at[n, chip],
+            device_id={"slot": 2 * k + core}, device_id_type=MESH,
+        )
+        pl.when(chip != k)(getattr(copy, step))
+
+    sums = {}
+    for low in range(0, PIECE if HI_AHEAD else 0, 8):
+        at = low // SPAN * 2 * SPAN + low % SPAN
+        sums[low] = combine(low, at, (steps, diffs), hi_recv, SPAN, grad_coeff * grad_v[low : low + 8, :])
     for n in range(PARTS):
         net.receive(*lo_copies[n])
         for low in range(CUTS[n], CUTS[n + 1], 8):
-            acc = grad_coeff * grad_v[low : low + 8, :]
             at = low // TILE * 2 * TILE + low % TILE
-            up = low // SPAN * 2 * SPAN + low % SPAN
-            for k in range(SLOTS):
-                s = hi_recv[k, up : up + 8, :].astype(F32) + lo_recv[k, at : at + 8, :].astype(F32)
-                y = hi_recv[k, up + SPAN : up + SPAN + 8, :].astype(F32)
-                y = y + lo_recv[k, at + TILE : at + TILE + 8, :].astype(F32)
-                acc = acc + steps[k] * s + diffs[k] * y
+            acc = combine(low, at, (steps, diffs), lo_recv, TILE, sums[low])
             out_ref[pl.ds(pl.multiple_of(me * PIECE + low, 8), 8), :] = acc
-        for i, (dz, flip) in enumerate(SPREAD):
-            dir_copies[n, dz, flip] = net.send(
-                piece(me, n), piece(me, n), dir_ss.at[n, i], dir_rs.at[n, i], slot=along(dz, flip)
-            )
+        for k in ORDER:
+            each(k, n, "start")
+        net.send(piece(me, n), piece(me, n), pass_ss.at[n, chip], pass_rs.at[n, chip], slot=mate)
+    net.drain(*copies, *[c for part_copies in lo_copies for c in part_copies])
     for n in range(PARTS):
         for dz in PASS:
-            net.receive(dir_copies[n, dz, 0])
-            source = along(CHIPS - dz, 0)
-            net.send(piece(source, n), piece(source, n), pass_ss.at[n, dz], pass_rs.at[n, dz], slot=mate)
+            k = lax.rem(chip + CHIPS - dz, CHIPS)
+            source = 2 * k + core
+            pltpu.make_async_remote_copy(
+                piece(source, n), piece(source, n), dir_ss.at[n, k], dir_rs.at[n, k],
+                device_id={"slot": source}, device_id_type=MESH,
+            ).wait_recv()
+            net.send(piece(source, n), piece(source, n), pass_ss.at[n, k], pass_rs.at[n, k], slot=mate)
+    for n in range(PARTS):
+        for k in ORDER:
+            each(k, n, "wait_send")
+    for n in range(PARTS):
+        for dz in (0, *PASS):
+            k = lax.rem(chip + CHIPS - dz, CHIPS)
+            other = 2 * k + 1 - core
+            pltpu.make_async_remote_copy(
+                piece(other, n), piece(other, n), pass_ss.at[n, k], pass_rs.at[n, k],
+                device_id={"slot": mate}, device_id_type=MESH,
+            ).wait_recv()
+    net.open = []
     net.finish()
 
 
@@ -331,8 +369,7 @@
             *[dma((PARTS, SLOTS))] * 2,
             *[dma((len(PLANE),))] * 2,
             *[dma((len(RING_SUM),))] * 2,
-            *[dma((PARTS, len(SPREAD)))] * 2,
-            *[dma((PARTS, CHIPS))] * 2,
+            *[dma((PARTS, CHIPS))] * 4,
         ],
         compiler_params=pltpu.CompilerParams(
             collective_id=0, has_side_effects=True, vmem_limit_bytes=VMEM_LIMIT

time: 48.9 us -> 47.5 us (0.971)
  Pallas kernels: 48.2 us -> 46.8 us
    pallas_call x1, Pallas kernels: 47.4 us -> 46 us  [call(): pl.pallas_call(kernel, out_shape=(pltpu.VMEM((ROWS, LANES), F32), pltpu.V...]
where the time goes in v3:
time: 47.5 us
  Pallas kernels  46.8 us (99%)
  between operations  0.64 us (1%)
    pallas_call x1, Pallas kernels, call(): pl.pallas_call(kernel, out_shape=(pltpu.VMEM((ROWS, LANES), F32), pltpu.V...  46 us

profile of v3, /device:TPU:1, one launch (start us, length us, event | category | flops | bytes accessed | tf_op | source)
XLA Modules:
  0.0 47.5 jit_solution(17883054738051697457)
XLA Ops:
  0.6 46.0 %lbfgs.1 = (f32[1024,128]{1,0:T(8,128)S(1)}, f32[33,33]{1,0:T(8,128)S(1)}) custom-call(f32[1024,128]{1,0:T(8,128)} %bitcast.4, f32[1024,128]{1,0:T(8,128)} %bitcast.5, f32[1024,128]{1,0:T(8,128)} %bitcast.6), custom_call_target="tpu_custom_call" | custom-call | tf_op jit(solution)/shard_map/lbfgs/pallas_call | solution.py:348
  46.6 0.8 %store.1 = (f32[1024,128]{1,0:T(8,128)}, f32[33,33]{1,0:T(8,128)}) custom-call(f32[1024,128]{1,0:T(8,128)S(1)} %get-tuple-element.6.direction_v, f32[33,33]{1,0:T(8,128)S(1)} %get-tuple-element.7.gram_v), custom_call_target="tpu_custom_call" | custom-call | tf_op jit(solution)/shard_map/store/pallas_call | solution.py:393

commit v4 on v3

--- a/solution.py
+++ b/solution.py
@@ -19,11 +19,8 @@
 MESH = pl.DeviceIdType.MESH
 SIDE = 4
 CHIPS = SLOTS // 2
-MERGED = True
-EARLY_DRAIN = True
-HI_AHEAD = True
+STORES = 1
 VMEM_LIMIT = 56 * 2**20
-HI_DRAIN = True
 LOADS_FIRST = 0
 RING_FIRST = True
 CORES_IN_PLANE = False
@@ -31,8 +28,10 @@
 HI_PARTS = 1
 SPAN = PIECE // HI_PARTS
 CUTS = (0, 16, 64)
+LO_CUTS = (0, 32, 128)
 LO_EARLY = 1
 PARTS = len(CUTS) - 1
+LO_PARTS = len(LO_CUTS) - 1
 
 
 def hops(offset, around):
@@ -175,9 +174,8 @@
         for copy in loads[dz]:
             copy.start()
     barrier = pltpu.get_barrier_semaphore()
-    peers = [(hops(dz, CHIPS), {"slot": along(dz, flip)}) for dz, flip in RING]
-    peers += [(hops(dx, SIDE) + hops(dy, SIDE), across(dx, dy, flip)) for dx, dy, flip in PLANE]
-    peers = [peer for _, peer in sorted(peers, key=lambda p: -p[0])] if MERGED else [peer for _, peer in peers]
+    peers = [{"slot": along(dz, flip)} for dz, flip in RING]
+    peers += [across(dx, dy, flip) for dx, dy, flip in PLANE]
     for peer in peers:
         pl.semaphore_signal(barrier, inc=1, device_id=peer, device_id_type=MESH)
     for dz in HOPS[LOADS_FIRST:]:
@@ -213,18 +211,22 @@
                 v = source[k * PIECE + row : k * PIECE + row + TILE, :]
                 lo_send[k, 2 * row + half : 2 * row + half + TILE, :] = (v - v.astype(BF16).astype(F32)).astype(BF16)
 
+    def together(ref, send_sem, recv_sem):
+        return pltpu.make_async_remote_copy(
+            ref, ref, send_sem, recv_sem, device_id={"slot": mate}, device_id_type=MESH
+        )
+
     def send_lo(part):
-        rows = pl.ds(2 * CUTS[part], 2 * (CUTS[part + 1] - CUTS[part]))
-        copies = []
-        for i, offset in enumerate(RING):
+        rows = pl.ds(LO_CUTS[part], LO_CUTS[part + 1] - LO_CUTS[part])
+        for offset in RING:
             dest = along(*offset)
-            copies.append(
-                net.send(lo_send.at[dest, rows], lo_recv.at[me, rows], lo_ss.at[part, i], lo_rs.at[part, i], slot=dest)
-            )
-        return copies
-
-    if HI_DRAIN:
-        net.drain(*[c for c in hi_copies if any(c is o for o in net.sent)])
+            pltpu.make_async_remote_copy(
+                lo_send.at[dest, rows], lo_recv.at[me, rows], lo_ss.at[part], lo_rs.at[part],
+                device_id={"slot": dest}, device_id_type=MESH,
+            ).start()
+        return together(lo_recv.at[pl.ds(0, len(RING)), rows], lo_ss.at[part], lo_rs.at[part])
+
+    net.drain(*hi_copies)
     lo_copies = [send_lo(part) for part in range(LO_EARLY)]
     lo_recv[me] = lo_send[me]
     grad_load.wait()
@@ -275,14 +277,13 @@
         stages.reverse()
     copies = exchange(packed, 0, *stages[0])
     if RING_FIRST:
-        lo_copies += [send_lo(part) for part in range(LO_EARLY, PARTS)]
+        lo_copies += [send_lo(part) for part in range(LO_EARLY, LO_PARTS)]
     net.receive(*reversed(copies))
     first = copies
     copies = exchange(total(stages[0][0]), 1, *stages[1])
-    if EARLY_DRAIN:
-        net.drain(*first)
+    net.drain(*first)
     if not RING_FIRST:
-        lo_copies += [send_lo(part) for part in range(LO_EARLY, PARTS)]
+        lo_copies += [send_lo(part) for part in range(LO_EARLY, LO_PARTS)]
     net.receive(*reversed(copies))
     gram = unpack(total(stages[1][0]) * (1.0 / (ROWS * LANES * COLS)))
     gram_ref[...] = gram[: 2 * HIST + 1, : 2 * HIST + 1]
@@ -298,49 +299,53 @@
             acc = acc + coeffs[1][k] * source[k, at + span : at + span + 8, :].astype(F32)
         return acc
 
-    def each(k, n, step):
+    def send_piece(k, n):
         copy = pltpu.make_async_remote_copy(
-            piece(me, n), piece(me, n), dir_ss.at[n, k], dir_rs.at[n, chip],
+            piece(me, n), piece(me, n), dir_ss.at[n], dir_rs.at[n, chip],
             device_id={"slot": 2 * k + core}, device_id_type=MESH,
         )
-        pl.when(chip != k)(getattr(copy, step))
+        pl.when(chip != k)(copy.start)
+
+    def pass_on(source, n):
+        pltpu.make_async_remote_copy(
+            piece(source, n), piece(source, n), pass_ss.at[n], pass_rs.at[n],
+            device_id={"slot": mate}, device_id_type=MESH,
+        ).start()
+
+    def pieces(number, n):
+        return out_ref.at[pl.ds(0, number * (CUTS[n + 1] - CUTS[n]))]
 
     sums = {}
-    for low in range(0, PIECE if HI_AHEAD else 0, 8):
+    for low in range(0, PIECE, 8):
         at = low // SPAN * 2 * SPAN + low % SPAN
         sums[low] = combine(low, at, (steps, diffs), hi_recv, SPAN, grad_coeff * grad_v[low : low + 8, :])
     for n in range(PARTS):
-        net.receive(*lo_copies[n])
+        arrived = sum(low < 2 * CUTS[n] for low in LO_CUTS[:-1]) if n else 0
+        needed = sum(low < 2 * CUTS[n + 1] for low in LO_CUTS[:-1])
+        for part in range(arrived, needed):
+            lo_copies[part].wait_recv()
         for low in range(CUTS[n], CUTS[n + 1], 8):
             at = low // TILE * 2 * TILE + low % TILE
             acc = combine(low, at, (steps, diffs), lo_recv, TILE, sums[low])
             out_ref[pl.ds(pl.multiple_of(me * PIECE + low, 8), 8), :] = acc
         for k in ORDER:
-            each(k, n, "start")
-        net.send(piece(me, n), piece(me, n), pass_ss.at[n, chip], pass_rs.at[n, chip], slot=mate)
-    net.drain(*copies, *[c for part_copies in lo_copies for c in part_copies])
+            send_piece(k, n)
+        pass_on(me, n)
+    net.drain(*copies)
+    for copy in lo_copies:
+        copy.wait_send()
     for n in range(PARTS):
         for dz in PASS:
             k = lax.rem(chip + CHIPS - dz, CHIPS)
             source = 2 * k + core
-            pltpu.make_async_remote_copy(
-                piece(source, n), piece(source, n), dir_ss.at[n, k], dir_rs.at[n, k],
-                device_id={"slot": source}, device_id_type=MESH,
-            ).wait_recv()
-            net.send(piece(source, n), piece(source, n), pass_ss.at[n, k], pass_rs.at[n, k], slot=mate)
+            together(piece(source, n), dir_ss.at[n], dir_rs.at[n, k]).wait_recv()
+            pass_on(source, n)
+    net.finish()
     for n in range(PARTS):
-        for k in ORDER:
-            each(k, n, "wait_send")
+        together(pieces(CHIPS - 1, n), dir_ss.at[n], pass_rs.at[n]).wait_send()
+        together(pieces(CHIPS, n), pass_ss.at[n], pass_rs.at[n]).wait_send()
     for n in range(PARTS):
-        for dz in (0, *PASS):
-            k = lax.rem(chip + CHIPS - dz, CHIPS)
-            other = 2 * k + 1 - core
-            pltpu.make_async_remote_copy(
-                piece(other, n), piece(other, n), pass_ss.at[n, k], pass_rs.at[n, k],
-                device_id={"slot": mate}, device_id_type=MESH,
-            ).wait_recv()
-    net.open = []
-    net.finish()
+        together(pieces(CHIPS, n), pass_ss.at[n], pass_rs.at[n]).wait_recv()
 
 
 def call(step, diff, grad):
@@ -366,10 +371,12 @@
             dma((2, CHIPS)),
             dma((1,)),
             *[dma((HI_PARTS, SLOTS))] * 2,
-            *[dma((PARTS, SLOTS))] * 2,
+            *[dma((LO_PARTS,))] * 2,
             *[dma((len(PLANE),))] * 2,
             *[dma((len(RING_SUM),))] * 2,
-            *[dma((PARTS, CHIPS))] * 4,
+            dma((PARTS,)),
+            dma((PARTS, CHIPS)),
+            *[dma((PARTS,))] * 2,
         ],
         compiler_params=pltpu.CompilerParams(
             collective_id=0, has_side_effects=True, vmem_limit_bytes=VMEM_LIMIT
@@ -379,10 +386,10 @@
 
 
 def write(direction_v, gram_v, direction_hbm, gram_hbm, sem):
-    copies = [
-        pltpu.make_async_copy(direction_v, direction_hbm, sem.at[0]),
-        pltpu.make_async_copy(gram_v, gram_hbm, sem.at[1]),
-    ]
+    copies = [pltpu.make_async_copy(gram_v, gram_hbm, sem.at[STORES])]
+    for i in range(STORES):
+        rows = pl.ds(i * ROWS // STORES, ROWS // STORES)
+        copies.append(pltpu.make_async_copy(direction_v.at[rows], direction_hbm.at[rows], sem.at[i]))
     for copy in copies:
         copy.start()
     for copy in copies:
@@ -398,7 +405,7 @@
         ),
         in_specs=[pl.BlockSpec(memory_space=pltpu.VMEM)] * 2,
         out_specs=(pl.BlockSpec(memory_space=pl.ANY), pl.BlockSpec(memory_space=pl.ANY)),
-        scratch_shapes=[pltpu.SemaphoreType.DMA((2,))],
+        scratch_shapes=[pltpu.SemaphoreType.DMA((STORES + 1,))],
         compiler_params=pltpu.CompilerParams(vmem_limit_bytes=2**20),
         name="store",
     )(direction, gram)

time: 47.5 us -> 46.5 us (0.979)
  Pallas kernels: 46.8 us -> 45.8 us
    pallas_call x1, Pallas kernels: 46 us -> 45 us  [call(): pl.pallas_call(kernel, out_shape=(pltpu.VMEM((ROWS, LANES), F32), pltpu.V...]
where the time goes in v4:
time: 46.5 us; the launch traced here: 46.4 us
  Pallas kernels  45.8 us (98%)
  between operations  0.64 us (1%)
    pallas_call x1, Pallas kernels, call(): pl.pallas_call(kernel, out_shape=(pltpu.VMEM((ROWS, LANES), F32), pltpu.V...  45 us

profile of v4, /device:TPU:1, one launch (start us, length us, event | category | flops | bytes accessed | tf_op | source)
XLA Modules:
  0.0 46.4 jit_solution(4227468820233910407)
XLA Ops:
  0.6 45.0 %lbfgs.1 = (f32[1024,128]{1,0:T(8,128)S(1)}, f32[33,33]{1,0:T(8,128)S(1)}) custom-call(f32[1024,128]{1,0:T(8,128)} %bitcast.4, f32[1024,128]{1,0:T(8,128)} %bitcast.5, f32[1024,128]{1,0:T(8,128)} %bitcast.6), custom_call_target="tpu_custom_call" | custom-call | tf_op jit(solution)/shard_map/lbfgs/pallas_call | solution.py:353
  45.6 0.8 %store.1 = (f32[1024,128]{1,0:T(8,128)}, f32[33,33]{1,0:T(8,128)}) custom-call(f32[1024,128]{1,0:T(8,128)S(1)} %get-tuple-element.6.direction_v, f32[33,33]{1,0:T(8,128)S(1)} %get-tuple-element.7.gram_v), custom_call_target="tpu_custom_call" | custom-call | tf_op jit(solution)/shard_map/store/pallas_call | solution.py:400

commit v5 on v4

--- a/solution.py
+++ b/solution.py
@@ -110,42 +110,11 @@
     return steps, diffs, -scale
 
 
-class Net:
-    def __init__(self):
-        self.sent, self.open, self.local = [], [], []
-
-    def send(self, source, target, send_sem, recv_sem, **peer):
-        copy = pltpu.make_async_remote_copy(
-            source, target, send_sem, recv_sem, device_id=peer, device_id_type=MESH
-        )
-        copy.start()
-        self.sent.append(copy)
-        self.open.append(copy)
-        return copy
-
-    def receive(self, *copies):
-        for copy in copies:
-            copy.wait_recv()
-            self.open = [c for c in self.open if c is not copy]
-
-    def drain(self, *copies):
-        for copy in copies:
-            copy.wait_send()
-            self.sent = [c for c in self.sent if c is not copy]
-
-    def finish(self):
-        for copy in self.local:
-            copy.wait()
-        self.receive(*list(self.open))
-        self.drain(*list(self.sent))
-
-
 def kernel(
     step_hbm, diff_hbm, grad_hbm, out_ref, gram_ref,
     step_v, diff_v, grad_v, hi_send, lo_send, hi_recv, lo_recv, wide, square, staged, plane_parts, ring_parts,
     load_sem, grad_sem, hi_ss, hi_rs, lo_ss, lo_rs, plane_ss, plane_rs, ring_ss, ring_rs, dir_ss, dir_rs, pass_ss, pass_rs,
 ):
-    net = Net()
     me = lax.axis_index("slot")
     col = lax.axis_index("param")
     mate = me + 1 - 2 * lax.rem(me, 2)
@@ -168,7 +137,6 @@
         ]
 
     loads = {dz: load(dz) for dz in HOPS}
-    net.local = [c for dz in HOPS for c in loads[dz]]
     grad_load = pltpu.make_async_copy(grad_hbm.at[own_rows], grad_v, grad_sem.at[0])
     for dz in HOPS[:LOADS_FIRST]:
         for copy in loads[dz]:
@@ -182,7 +150,6 @@
         for copy in loads[dz]:
             copy.start()
     grad_load.start()
-    net.local.append(grad_load)
     pl.semaphore_wait(barrier, len(peers))
     hi_copies = []
     for part in range(HI_PARTS):
@@ -191,15 +158,17 @@
             if not part and (not flip or not dz):
                 for copy in loads[dz]:
                     copy.wait()
-                    net.local = [c for c in net.local if c is not copy]
             dest = along(dz, flip)
             for half, source in ((0, step_v), (SPAN, diff_v)):
                 v = source[pl.ds(pl.multiple_of(dest * PIECE + part * SPAN, 8), SPAN), :]
                 at = 2 * SPAN * part + half
                 hi_send[dest, at : at + SPAN, :] = v.astype(BF16)
-            hi_copies.append(
-                net.send(hi_send.at[dest, rows], hi_recv.at[me, rows], hi_ss.at[part, i], hi_rs.at[part, i], slot=dest)
+            copy = pltpu.make_async_remote_copy(
+                hi_send.at[dest, rows], hi_recv.at[me, rows], hi_ss.at[part], hi_rs.at[part, i],
+                device_id={"slot": dest}, device_id_type=MESH,
             )
+            copy.start()
+            hi_copies.append(copy)
         for half, source in ((0, step_v), (SPAN, diff_v)):
             v = source[pl.ds(pl.multiple_of(me * PIECE + part * SPAN, 8), SPAN), :]
             at = 2 * SPAN * part + half
@@ -226,11 +195,12 @@
             ).start()
         return together(lo_recv.at[pl.ds(0, len(RING)), rows], lo_ss.at[part], lo_rs.at[part])
 
-    net.drain(*hi_copies)
+    for part in range(HI_PARTS):
+        rows = pl.ds(2 * SPAN * part, 2 * SPAN)
+        together(hi_recv.at[pl.ds(0, len(RING)), rows], hi_ss.at[part], hi_rs.at[part, 0]).wait_send()
     lo_copies = [send_lo(part) for part in range(LO_EARLY)]
     lo_recv[me] = lo_send[me]
     grad_load.wait()
-    net.local = []
     wide[2 * HIST * STRIDE : 2 * HIST * STRIDE + PIECE, :] = grad_v[...].astype(BF16).astype(F32)
     for j in range(2 * HIST + 1, VECS):
         wide[j * STRIDE : j * STRIDE + PIECE, :] = jnp.zeros((PIECE, LANES), F32)
@@ -245,7 +215,7 @@
     for part in range(HI_PARTS):
         widen(me, part)
         for i, (dz, flip) in enumerate(RING):
-            net.receive(hi_copies[part * len(RING) + i])
+            hi_copies[part * len(RING) + i].wait_recv()
             widen(along(CHIPS - dz, flip), part)
         rows = [wide[pl.ds(r, VECS, stride=STRIDE), :].astype(BF16) for r in range(part * SPAN, (part + 1) * SPAN)]
         flat = jnp.concatenate(rows, axis=1)
@@ -257,10 +227,12 @@
     def exchange(value, number, parts, mine, peers, send_sems, recv_sems):
         staged[number] = value
         parts[mine] = value
-        return [
-            net.send(staged.at[number], parts.at[mine], send_sems.at[i], recv_sems.at[i], **peer)
-            for i, peer in enumerate(peers)
-        ]
+        for peer in peers:
+            pltpu.make_async_remote_copy(
+                staged.at[number], parts.at[mine], send_sems.at[0], recv_sems.at[0],
+                device_id=peer, device_id_type=MESH,
+            ).start()
+        return together(parts.at[pl.ds(0, len(peers))], send_sems.at[0], recv_sems.at[0])
 
     def total(parts):
         values = [parts[k] for k in range(parts.shape[0])]
@@ -278,13 +250,13 @@
     copies = exchange(packed, 0, *stages[0])
     if RING_FIRST:
         lo_copies += [send_lo(part) for part in range(LO_EARLY, LO_PARTS)]
-    net.receive(*reversed(copies))
+    copies.wait_recv()
     first = copies
     copies = exchange(total(stages[0][0]), 1, *stages[1])
-    net.drain(*first)
+    first.wait_send()
     if not RING_FIRST:
         lo_copies += [send_lo(part) for part in range(LO_EARLY, LO_PARTS)]
-    net.receive(*reversed(copies))
+    copies.wait_recv()
     gram = unpack(total(stages[1][0]) * (1.0 / (ROWS * LANES * COLS)))
     gram_ref[...] = gram[: 2 * HIST + 1, : 2 * HIST + 1]
     steps, diffs, grad_coeff = recursion(gram)
@@ -331,7 +303,7 @@
         for k in ORDER:
             send_piece(k, n)
         pass_on(me, n)
-    net.drain(*copies)
+    copies.wait_send()
     for copy in lo_copies:
         copy.wait_send()
     for n in range(PARTS):
@@ -340,7 +312,6 @@
             source = 2 * k + core
             together(piece(source, n), dir_ss.at[n], dir_rs.at[n, k]).wait_recv()
             pass_on(source, n)
-    net.finish()
     for n in range(PARTS):
         together(pieces(CHIPS - 1, n), dir_ss.at[n], pass_rs.at[n]).wait_send()
         together(pieces(CHIPS, n), pass_ss.at[n], pass_rs.at[n]).wait_send()
@@ -370,10 +341,10 @@
             pltpu.VMEM((len(RING_SUM) + 1, 8, LANES), F32),
             dma((2, CHIPS)),
             dma((1,)),
-            *[dma((HI_PARTS, SLOTS))] * 2,
+            dma((HI_PARTS,)),
+            dma((HI_PARTS, SLOTS)),
             *[dma((LO_PARTS,))] * 2,
-            *[dma((len(PLANE),))] * 2,
-            *[dma((len(RING_SUM),))] * 2,
+            *[dma((1,))] * 4,
             dma((PARTS,)),
             dma((PARTS, CHIPS)),
             *[dma((PARTS,))] * 2,

time: 46.5 us -> 46.1 us (level)
  no operation moved by 1% of the time
where the time goes in v5:
time: 46.1 us; the launch traced here: 46 us
  Pallas kernels  45.4 us (98%)
  between operations  0.64 us (1%)
    pallas_call x1, Pallas kernels, call(): pl.pallas_call(kernel, out_shape=(pltpu.VMEM((ROWS, LANES), F32), pltpu.V...  44.5 us

profile of v5, /device:TPU:1, one launch (start us, length us, event | category | flops | bytes accessed | tf_op | source)
XLA Modules:
  0.0 46.0 jit_solution(696400838166210287)
XLA Ops:
  0.6 44.5 %lbfgs.1 = (f32[1024,128]{1,0:T(8,128)S(1)}, f32[33,33]{1,0:T(8,128)S(1)}) custom-call(f32[1024,128]{1,0:T(8,128)} %bitcast.4, f32[1024,128]{1,0:T(8,128)} %bitcast.5, f32[1024,128]{1,0:T(8,128)} %bitcast.6), custom_call_target="tpu_custom_call" | custom-call | tf_op jit(solution)/shard_map/lbfgs/pallas_call | solution.py:324
  45.2 0.8 %store.1 = (f32[1024,128]{1,0:T(8,128)}, f32[33,33]{1,0:T(8,128)}) custom-call(f32[1024,128]{1,0:T(8,128)S(1)} %get-tuple-element.6.direction_v, f32[33,33]{1,0:T(8,128)S(1)} %get-tuple-element.7.gram_v), custom_call_target="tpu_custom_call" | custom-call | tf_op jit(solution)/shard_map/store/pallas_call | solution.py:371

commit v6 on v5

--- a/solution.py
+++ b/solution.py
@@ -265,10 +265,13 @@
         start = pl.multiple_of(slot * PIECE + CUTS[part], 8)
         return out_ref.at[pl.ds(start, CUTS[part + 1] - CUTS[part])]
 
-    def combine(row, at, coeffs, source, span, acc):
+    steps, diffs = ([jnp.concatenate([c, c], axis=0) for c in side] for side in (steps, diffs))
+    grad_coeff = jnp.concatenate([grad_coeff, grad_coeff], axis=0)
+
+    def combine(at, source, span, acc):
         for k in range(SLOTS):
-            acc = acc + coeffs[0][k] * source[k, at : at + 8, :].astype(F32)
-            acc = acc + coeffs[1][k] * source[k, at + span : at + span + 8, :].astype(F32)
+            acc = acc + steps[k] * source[k, at : at + TILE, :].astype(F32)
+            acc = acc + diffs[k] * source[k, at + span : at + span + TILE, :].astype(F32)
         return acc
 
     def send_piece(k, n):
@@ -288,18 +291,16 @@
         return out_ref.at[pl.ds(0, number * (CUTS[n + 1] - CUTS[n]))]
 
     sums = {}
-    for low in range(0, PIECE, 8):
+    for low in range(0, PIECE, TILE):
         at = low // SPAN * 2 * SPAN + low % SPAN
-        sums[low] = combine(low, at, (steps, diffs), hi_recv, SPAN, grad_coeff * grad_v[low : low + 8, :])
+        sums[low] = combine(at, hi_recv, SPAN, grad_coeff * grad_v[low : low + TILE, :])
     for n in range(PARTS):
         arrived = sum(low < 2 * CUTS[n] for low in LO_CUTS[:-1]) if n else 0
         needed = sum(low < 2 * CUTS[n + 1] for low in LO_CUTS[:-1])
         for part in range(arrived, needed):
             lo_copies[part].wait_recv()
-        for low in range(CUTS[n], CUTS[n + 1], 8):
-            at = low // TILE * 2 * TILE + low % TILE
-            acc = combine(low, at, (steps, diffs), lo_recv, TILE, sums[low])
-            out_ref[pl.ds(pl.multiple_of(me * PIECE + low, 8), 8), :] = acc
+        for low in range(CUTS[n], CUTS[n + 1], TILE):
+            out_ref[pl.ds(pl.multiple_of(me * PIECE + low, TILE), TILE), :] = combine(2 * low, lo_recv, TILE, sums[low])
         for k in ORDER:
             send_piece(k, n)
         pass_on(me, n)

time: 46.1 us -> 46.1 us (level)
  no operation moved by 1% of the time
where the time goes in v6:
time: 46.1 us; the launch traced here: 46 us
  Pallas kernels  45.4 us (98%)
  between operations  0.64 us (1%)
    pallas_call x1, Pallas kernels, call(): pl.pallas_call(kernel, out_shape=(pltpu.VMEM((ROWS, LANES), F32), pltpu.V...  44.5 us

profile of v6, /device:TPU:1, one launch (start us, length us, event | category | flops | bytes accessed | tf_op | source)
XLA Modules:
  0.0 46.0 jit_solution(3608318727753023319)
XLA Ops:
  0.6 44.5 %lbfgs.1 = (f32[1024,128]{1,0:T(8,128)S(1)}, f32[33,33]{1,0:T(8,128)S(1)}) custom-call(f32[1024,128]{1,0:T(8,128)} %bitcast.4, f32[1024,128]{1,0:T(8,128)} %bitcast.5, f32[1024,128]{1,0:T(8,128)} %bitcast.6), custom_call_target="tpu_custom_call" | custom-call | tf_op jit(solution)/shard_map/lbfgs/pallas_call | solution.py:325
  45.2 0.8 %store.1 = (f32[1024,128]{1,0:T(8,128)}, f32[33,33]{1,0:T(8,128)}) custom-call(f32[1024,128]{1,0:T(8,128)S(1)} %get-tuple-element.6.direction_v, f32[33,33]{1,0:T(8,128)S(1)} %get-tuple-element.7.gram_v), custom_call_target="tpu_custom_call" | custom-call | tf_op jit(solution)/shard_map/store/pallas_call | solution.py:372

commit v7 on v6

--- a/solution.py
+++ b/solution.py
@@ -27,8 +27,8 @@
 TILE = 16
 HI_PARTS = 1
 SPAN = PIECE // HI_PARTS
-CUTS = (0, 16, 64)
-LO_CUTS = (0, 32, 128)
+CUTS = (0, 32, 64)
+LO_CUTS = (0, 32, 64, 128)
 LO_EARLY = 1
 PARTS = len(CUTS) - 1
 LO_PARTS = len(LO_CUTS) - 1
@@ -42,7 +42,7 @@
 RING = [(dz, flip) for dz in HOPS for flip in (0, 1) if dz or flip]
 RING_SUM = [(dz, flip) for dz, flip in RING if not (CORES_IN_PLANE and (flip or not dz))]
 ORDER = (0, 4, 1, 5, 2, 6, 3, 7)
-PASS = (4, 3, 5, 2, 6, 1, 7)
+PASS = (1, 7, 2, 6, 3, 5, 4)
 PLANE = sorted(
     ((x, y, flip) for x in range(SIDE) for y in range(SIDE) for flip in range(1 + CORES_IN_PLANE) if x or y or flip),
     key=lambda o: (-hops(o[0], SIDE) - hops(o[1], SIDE), o),

time: 46.1 us -> 46 us (level)
  no operation moved by 1% of the time
where the time goes in v7:
time: 46 us; the launch traced here: 45.9 us
  Pallas kernels  45.3 us (98%)
  between operations  0.64 us (1%)
    pallas_call x1, Pallas kernels, call(): pl.pallas_call(kernel, out_shape=(pltpu.VMEM((ROWS, LANES), F32), pltpu.V...  44.5 us

profile of v7, /device:TPU:1, one launch (start us, length us, event | category | flops | bytes accessed | tf_op | source)
XLA Modules:
  0.0 45.9 jit_solution(3786992581016903321)
XLA Ops:
  0.6 44.5 %lbfgs.1 = (f32[1024,128]{1,0:T(8,128)S(1)}, f32[33,33]{1,0:T(8,128)S(1)}) custom-call(f32[1024,128]{1,0:T(8,128)} %bitcast.4, f32[1024,128]{1,0:T(8,128)} %bitcast.5, f32[1024,128]{1,0:T(8,128)} %bitcast.6), custom_call_target="tpu_custom_call" | custom-call | tf_op jit(solution)/shard_map/lbfgs/pallas_call | solution.py:325
  45.1 0.8 %store.1 = (f32[1024,128]{1,0:T(8,128)}, f32[33,33]{1,0:T(8,128)}) custom-call(f32[1024,128]{1,0:T(8,128)S(1)} %get-tuple-element.6.direction_v, f32[33,33]{1,0:T(8,128)S(1)} %get-tuple-element.7.gram_v), custom_call_target="tpu_custom_call" | custom-call | tf_op jit(solution)/shard_map/store/pallas_call | solution.py:372
